TPU v7x, 32 devices: a whole 2x2x4 slice. The times are simulated.
32 devices in a mesh: temp: 2 (over y), row: 4 (over x, core), col: 4 (over z).
Axes of the slice: x: 2, y: 2, z: 4, core: 2. Of those that a mesh axis runs over, the one named last changes fastest.
Arguments:
- subspace: bfloat16 [32768, 128], P(('temp', 'row', 'col')), parts along dimension 0, may hold values from -6 to 6
- hamiltonian: bfloat16 [768, 512, 512], P(('temp', 'row', 'col')), parts along dimension 0
- tile_blocks: int32 [16, 24, 2], P(('row', 'col')), may hold values from 0 to 31, as said below
- tile_count: int32 [16], P(('row', 'col')), may hold values from 2 to 24, as said below
- cut_bound: float32 [2], P('temp'), parts along dimension 0, may hold values from -0.6 to 0.2
- top_bound: float32 [2], P('temp'), parts along dimension 0, may hold values from 2.2 to 3.2
Outputs:
- filtered_first: bfloat16 [32768, 128], P(('temp', 'row', 'col')), parts along dimension 0
- filtered: bfloat16 [32768, 128], P(('temp', 'row', 'col')), parts along dimension 0
There are 2 independent parts, one for each index of `temp`. A program takes and returns all parts, laid end to end along the dimension named above; an argument that names none is the same for every part. Nothing has to cross between parts.
Inputs may be any that keep to these rules, and one draw needn't show every extreme that they name: `tile_blocks`: for grid cell d = p * 4 + q, slots 0 to 1 hold the diagonal pairs (d * 2 + k, d * 2 + k); the other live slots hold distinct pairs (i, j) with i < j, p * 8 <= i < p * 8 + 8, and j = s * 8 + q * 2 + k with 0 <= k < 2; slots from tile_count[d] on repeat the first diagonal pair. `tile_count`: every cell of the first grid row holds 24 live tiles.
All inputs are finite; a program needn't handle non-finite values.
Results may differ from a plain program's by a relative error of at most 0.013.
Values may be sent and summed in bfloat16 or wider, within the bound.
A program may use at most 128 MiB of HBM per device.

v0:
```python
import jax
import jax.numpy as jnp
from jax import lax
from jax.sharding import PartitionSpec as P


def sum_rows(row_partial):
    return lax.psum_scatter(
        row_partial.astype(jnp.bfloat16), "col", scatter_dimension=0, tiled=True
    ).astype(jnp.float32)


def sum_columns(col_partial):
    return lax.psum_scatter(
        col_partial.astype(jnp.bfloat16), "row", scatter_dimension=0, tiled=True
    ).astype(jnp.float32)


def body(subspace, hamiltonian, tile_blocks, tile_count, cut_bound, top_bound):
    block_size = hamiltonian.shape[1]
    vec_width = subspace.shape[1]
    slot_total = hamiltonian.shape[0]
    per_device = subspace.shape[0] // block_size
    row_span = per_device * lax.axis_size("col")
    col_span = per_device * lax.axis_size("row")
    row_index = lax.axis_index("row")
    tile_pairs = tile_blocks[0]
    tile_total = tile_count[0]
    center = (cut_bound[0] + top_bound[0]) * 0.5
    half_width = (top_bound[0] - cut_bound[0]) * 0.5
    first_blocks = tile_pairs[:, 0]
    second_blocks = tile_pairs[:, 1]
    local_rows = first_blocks - row_index * row_span
    local_cols = second_blocks // row_span * per_device + second_blocks % per_device
    slot_ids = jnp.arange(slot_total, dtype=jnp.int32)
    is_live = slot_ids < tile_total
    is_upper = jnp.logical_and(is_live, first_blocks != second_blocks)
    row_table = jnp.logical_and(
        jnp.arange(row_span, dtype=jnp.int32)[:, None] == local_rows[None, :], is_live[None, :]
    ).astype(jnp.float32)
    col_table = jnp.logical_and(
        jnp.arange(col_span, dtype=jnp.int32)[:, None] == local_cols[None, :], is_upper[None, :]
    ).astype(jnp.float32)

    def row_terms(column_set):
        picked = jnp.take(column_set, local_cols, axis=0)
        products = jnp.einsum(
            "sij,sjn->sin", hamiltonian, picked, preferred_element_type=jnp.float32
        )
        summed = jnp.einsum("rs,sin->rin", row_table, products, precision=lax.Precision.HIGHEST)
        return summed.reshape(row_span * block_size, vec_width)

    def col_terms(row_set):
        picked = jnp.take(row_set, local_rows, axis=0)
        products = jnp.einsum(
            "sji,sjn->sin", hamiltonian, picked, preferred_element_type=jnp.float32
        )
        summed = jnp.einsum("rs,sin->rin", col_table, products, precision=lax.Precision.HIGHEST)
        return summed.reshape(col_span * block_size, vec_width)

    def apply_operator(vectors):
        column_set = lax.all_gather(vectors, "row", axis=0, tiled=True).reshape(
            col_span, block_size, vec_width
        )
        row_set = lax.all_gather(vectors, "col", axis=0, tiled=True).reshape(
            row_span, block_size, vec_width
        )
        row_partial = row_terms(column_set)
        col_partial = col_terms(row_set)
        summed_rows = sum_rows(row_partial)
        summed_cols = sum_columns(col_partial)
        return summed_rows + summed_cols

    vectors32 = subspace.astype(jnp.float32)
    image_one = apply_operator(subspace)
    filtered_first = ((image_one - center * vectors32) / half_width).astype(jnp.bfloat16)
    image_two = apply_operator(filtered_first)
    filtered = (
        2.0 / half_width * (image_two - center * filtered_first.astype(jnp.float32)) - vectors32
    ).astype(jnp.bfloat16)
    return (filtered_first, filtered)


def solution(mesh):
    return jax.shard_map(
        body,
        mesh=mesh,
        in_specs=(
            P(("temp", "row", "col"), None),
            P(("temp", "row", "col"), None, None),
            P(("row", "col"), None, None),
            P(("row", "col")),
            P("temp"),
            P("temp"),
        ),
        out_specs=(P(("temp", "row", "col"), None), P(("temp", "row", "col"), None)),
        check_vma=False,
    )
```

profile of v0, /device:TPU:0, one launch (start us, length us, event | category | flops | bytes accessed | tf_op | source)
XLA Modules:
  0.0 237.0 jit_solution(6268484649578034562)
XLA Ops:
  7.2 0.0 all-gather.7.cloned.1.call-start
  7.2 0.7 all-gather.7.cloned.1.call-update
  7.9 0.0 all-gather.5.cloned.1.call-start
  7.9 0.7 all-gather.5.cloned.1.call-update
  8.6 0.0 reduce-scatter.7.cloned.1.call-start
  9.3 0.8 compare_and_fusion.1
  10.1 30.1 %all-gather.7.cloned.1.call-done = bf16[4096,128]{1,0:T(8,128)(2,1)} async-done(((bf16[1024,128]{1,0:T(8,128)(2,1)}), bf16[4096,128]{1,0:T(8,128)(2,1)}) %all-gather.7.cloned.1.call-update) | async-done | bytes 1048592 | tf_op jit(solution)/shard_map/all_gather | solution.py:65
  40.2 2.4 %gather_fusion.1 = bf16[24,512,128]{2,1,0:T(8,128)(2,1)S(1)} fusion(bf16[8,512,128]{2,1,0:T(8,128)(2,1)} %bitcast.64, s32[1024]{0:T(1024)S(1)} %pad_clamp_fusion), kind=kCustom, calls=%fused_computation.1.clone | custom fusion | bytes 6291552 | tf_op jit(solution)/shard_map/jit(_take)/gather | solution.py:54
  42.6 9.8 %fusion.12 = f32[24,128,512]{2,1,0:T(8,128)} fusion(bf16[24,512,512]{2,1,0:T(8,128)(2,1)} %param.9, bf16[24,512,128]{2,1,0:T(8,128)(2,1)S(1)} %gather_fusion.1, pred[24]{0:T(512)(128)(4,1)S(1)} %get-tuple-element.8), kind=kOutput, calls=%fused_computation.16 | convolution fusion | flops 1612185600 | bytes 22020120 | tf_op jit(solution)/shard_map/sji,sjn->sin/dot_general | solution.py:55
  52.4 6.6 %copy.13 = f32[24,128,512]{1,0,2:T(8,128)} copy(f32[24,128,512]{2,1,0:T(8,128)} %fusion.12) | data formatting | bytes 12582912 | tf_op jit(solution)/shard_map/sji,sjn->sin/dot_general | solution.py:55
  59.0 5.1 %fusion.27 = bf16[8,512,128]{2,0,1:T(8,128)(2,1)S(1)} fusion(f32[24,128,512]{1,0,2:T(8,128)} %copy.13, s32[24]{0:T(128)S(1)} %get-tuple-element.4, pred[24]{0:T(512)(128)(4,1)S(1)} %get-tuple-element.7), kind=kOutput, calls=%fused_computation.29 | convolution fusion | flops 151519616 | bytes 7340152 | tf_op jit(solution)/shard_map/rs,sin->rin/dot_general | solution.py:58
  64.0 1.2 copy.9
  65.3 0.0 reduce-scatter.7.cloned.1.call-update
  65.3 0.2 reduce-scatter.5.cloned.1.call-start
  65.5 0.0 all-gather.5.cloned.1.call-done
  65.6 2.4 %gather_fusion = bf16[24,512,128]{2,1,0:T(8,128)(2,1)S(1)} fusion(bf16[8,512,128]{2,1,0:T(8,128)(2,1)} %bitcast.63, s32[1024]{0:T(1024)S(1)} %pad_clamp_fusion.1), kind=kCustom, calls=%fused_computation.clone | custom fusion | bytes 6291552 | tf_op jit(solution)/shard_map/jit(_take)/gather | solution.py:46
  68.0 12.5 %fusion.14 = f32[24,128,512]{2,1,0:T(8,128)} fusion(bf16[24,512,512]{2,1,0:T(8,128)(2,1)} %param.9, bf16[24,512,128]{2,1,0:T(8,128)(2,1)S(1)} %gather_fusion, pred[24]{0:T(512)(128)(4,1)S(1)} %get-tuple-element.3), kind=kOutput, calls=%fused_computation.18 | convolution fusion | flops 1612185600 | bytes 22020120 | tf_op jit(solution)/shard_map/sij,sjn->sin/dot_general | solution.py:47
  80.5 6.7 %copy.12 = f32[24,128,512]{1,0,2:T(8,128)} copy(f32[24,128,512]{2,1,0:T(8,128)} %fusion.14) | data formatting | bytes 12582912 | tf_op jit(solution)/shard_map/sij,sjn->sin/dot_general | solution.py:47
  87.1 5.1 %fusion.24 = bf16[8,512,128]{2,0,1:T(8,128)(2,1)S(1)} fusion(f32[24,128,512]{1,0,2:T(8,128)} %copy.12, s32[24]{0:T(128)S(1)} %get-tuple-element.9, pred[24]{0:T(512)(128)(4,1)S(1)} %iota_compare_fusion.2), kind=kOutput, calls=%fused_computation.28 | convolution fusion | flops 151519616 | bytes 7340152 | tf_op jit(solution)/shard_map/rs,sin->rin/dot_general | solution.py:50
  92.2 1.1 copy.8
  93.4 0.0 reduce-scatter.5.cloned.1.call-update
  93.4 0.0 all-gather.11.cloned.1.call-start
  94.8 0.0 reduce-scatter.7.cloned.1.call-done
  94.8 25.1 %reduce-scatter.5.cloned.1.call-done = bf16[1024,128]{1,0:T(8,128)(2,1)} async-done(((bf16[4096,128]{1,0:T(8,128)(2,1)}), bf16[1024,128]{1,0:T(8,128)(2,1)}) %reduce-scatter.5.cloned.1.call-update) | async-done | bytes 262160 | tf_op jit(solution)/shard_map/reduce_scatter | solution.py:8
  119.9 1.9 fusion.38
  121.8 0.0 all-gather.11.cloned.1.call-update
  121.8 0.0 all-gather.9.cloned.1.call-start
  121.8 0.5 all-gather.9.cloned.1.call-update
  122.4 0.3 reduce-scatter.11.cloned.1.call-start
  122.6 25.9 %all-gather.11.cloned.1.call-done = bf16[4096,128]{1,0:T(8,128)(2,1)} async-done(((bf16[1024,128]{1,0:T(8,128)(2,1)}), bf16[4096,128]{1,0:T(8,128)(2,1)}) %all-gather.11.cloned.1.call-update) | async-done | bytes 1048592 | tf_op jit(solution)/shard_map/all_gather | solution.py:65
  148.5 2.4 %gather_fusion.3 = bf16[24,512,128]{2,1,0:T(8,128)(2,1)S(1)} fusion(bf16[8,512,128]{2,1,0:T(8,128)(2,1)} %bitcast.66, s32[1024]{0:T(1024)S(1)} %pad_clamp_fusion), kind=kCustom, calls=%fused_computation.3.clone | custom fusion | bytes 6291552 | tf_op jit(solution)/shard_map/jit(_take)/gather | solution.py:54
  150.9 9.8 %fusion.8 = f32[24,128,512]{2,1,0:T(8,128)} fusion(bf16[24,512,512]{2,1,0:T(8,128)(2,1)} %param.9, bf16[24,512,128]{2,1,0:T(8,128)(2,1)S(1)} %gather_fusion.3, pred[24]{0:T(512)(128)(4,1)S(1)} %get-tuple-element.8), kind=kOutput, calls=%fused_computation.12 | convolution fusion | flops 1612185600 | bytes 22020120 | tf_op jit(solution)/shard_map/sji,sjn->sin/dot_general | solution.py:55
  160.7 6.6 %copy.15 = f32[24,128,512]{1,0,2:T(8,128)} copy(f32[24,128,512]{2,1,0:T(8,128)} %fusion.8) | data formatting | bytes 12582912 | tf_op jit(solution)/shard_map/sji,sjn->sin/dot_general | solution.py:55
  167.3 5.1 %fusion.33 = bf16[8,512,128]{2,0,1:T(8,128)(2,1)S(1)} fusion(f32[24,128,512]{1,0,2:T(8,128)} %copy.15, s32[24]{0:T(128)S(1)} %get-tuple-element.4, pred[24]{0:T(512)(128)(4,1)S(1)} %get-tuple-element.7), kind=kOutput, calls=%fused_computation.31 | convolution fusion | flops 151519616 | bytes 7340152 | tf_op jit(solution)/shard_map/rs,sin->rin/dot_general | solution.py:58
  172.3 1.2 copy.11
  173.6 0.0 reduce-scatter.11.cloned.1.call-update
  173.6 0.3 reduce-scatter.9.cloned.1.call-start
  173.9 0.0 all-gather.9.cloned.1.call-done
  173.9 2.4 %gather_fusion.2 = bf16[24,512,128]{2,1,0:T(8,128)(2,1)S(1)} fusion(bf16[8,512,128]{2,1,0:T(8,128)(2,1)} %bitcast.65, s32[1024]{0:T(1024)S(1)} %pad_clamp_fusion.1), kind=kCustom, calls=%fused_computation.2.clone | custom fusion | bytes 6291552 | tf_op jit(solution)/shard_map/jit(_take)/gather | solution.py:46
  176.3 12.5 %fusion.10 = f32[24,128,512]{2,1,0:T(8,128)} fusion(bf16[24,512,512]{2,1,0:T(8,128)(2,1)} %param.9, bf16[24,512,128]{2,1,0:T(8,128)(2,1)S(1)} %gather_fusion.2, pred[24]{0:T(512)(128)(4,1)S(1)} %get-tuple-element.3), kind=kOutput, calls=%fused_computation.14 | convolution fusion | flops 1612185600 | bytes 22020120 | tf_op jit(solution)/shard_map/sij,sjn->sin/dot_general | solution.py:47
  188.8 6.7 %copy.14 = f32[24,128,512]{1,0,2:T(8,128)} copy(f32[24,128,512]{2,1,0:T(8,128)} %fusion.10) | data formatting | bytes 12582912 | tf_op jit(solution)/shard_map/sij,sjn->sin/dot_general | solution.py:47
  195.5 5.1 %fusion.30 = bf16[8,512,128]{2,0,1:T(8,128)(2,1)S(1)} fusion(f32[24,128,512]{1,0,2:T(8,128)} %copy.14, s32[24]{0:T(128)S(1)} %get-tuple-element.9, pred[24]{0:T(512)(128)(4,1)S(1)} %iota_compare_fusion.2), kind=kOutput, calls=%fused_computation.30 | convolution fusion | flops 151519616 | bytes 7340152 | tf_op jit(solution)/shard_map/rs,sin->rin/dot_general | solution.py:50
  200.6 0.0 copy-start.1
  200.6 1.1 copy.10
  201.7 0.0 reduce-scatter.9.cloned.1.call-update
  201.8 0.0 reduce-scatter.11.cloned.1.call-done
  201.8 26.4 %reduce-scatter.9.cloned.1.call-done = bf16[1024,128]{1,0:T(8,128)(2,1)} async-done(((bf16[4096,128]{1,0:T(8,128)(2,1)}), bf16[1024,128]{1,0:T(8,128)(2,1)}) %reduce-scatter.9.cloned.1.call-update) | async-done | bytes 262160 | tf_op jit(solution)/shard_map/reduce_scatter | solution.py:8
  228.3 1.9 fusion.39
  (8 shorter events, 0.0 us)
Async XLA Ops:
  7.2 33.1 %all-gather.7.cloned.1.call-start = ((), (), s32[]{:S(2)}) async-start(), calls=%async_computation.6 | async-start | bytes 1310720 | tf_op jit(solution)/shard_map/all_gather | solution.py:65
  7.9 57.7 %all-gather.5.cloned.1.call-start = ((), (), s32[]{:S(2)}) async-start(), calls=%async_computation.4 | async-start | bytes 1310720 | tf_op jit(solution)/shard_map/all_gather | solution.py:62
  8.6 86.1 %reduce-scatter.7.cloned.1.call-start = ((), (), s32[]{:S(2)}) async-start(), calls=%async_computation.7 | async-start | bytes 1310720 | tf_op jit(solution)/shard_map/reduce_scatter | solution.py:14
  65.3 54.6 %reduce-scatter.5.cloned.1.call-start = ((), (), s32[]{:S(2)}) async-start(), calls=%async_computation.5 | async-start | bytes 1310720 | tf_op jit(solution)/shard_map/reduce_scatter | solution.py:8
  92.2 27.7 %copy-start = (bf16[1024,128]{1,0:T(8,128)(2,1)S(1)}, bf16[1024,128]{1,0:T(8,128)(2,1)}, u32[]{:S(2)}) copy-start(bf16[1024,128]{1,0:T(8,128)(2,1)} %param.8) | copy-start | bytes 786436
  93.4 55.1 %all-gather.11.cloned.1.call-start = ((), (), s32[]{:S(2)}) async-start(), calls=%async_computation.10 | async-start | bytes 1310720 | tf_op jit(solution)/shard_map/all_gather | solution.py:65
  121.8 52.1 %all-gather.9.cloned.1.call-start = ((), (), s32[]{:S(2)}) async-start(), calls=%async_computation.8 | async-start | bytes 1310720 | tf_op jit(solution)/shard_map/all_gather | solution.py:62
  122.4 79.4 %reduce-scatter.11.cloned.1.call-start = ((), (), s32[]{:S(2)}) async-start(), calls=%async_computation.11 | async-start | bytes 1310720 | tf_op jit(solution)/shard_map/reduce_scatter | solution.py:14
  173.6 54.7 %reduce-scatter.9.cloned.1.call-start = ((), (), s32[]{:S(2)}) async-start(), calls=%async_computation.9 | async-start | bytes 1310720 | tf_op jit(solution)/shard_map/reduce_scatter | solution.py:8
  200.6 27.7 %copy-start.1 = (bf16[1024,128]{1,0:T(8,128)(2,1)S(1)}, bf16[1024,128]{1,0:T(8,128)(2,1)}, u32[]{:S(2)}) copy-start(bf16[1024,128]{1,0:T(8,128)(2,1)} %fusion.38) | copy-start | bytes 786436
Sparse Core Ops, SparseCore 0:
  9.6 30.6 all-gather.6
  41.8 16.2 all-gather.4
  65.4 24.4 reduce-scatter.6
  93.5 26.3 reduce-scatter.4
  121.9 26.5 all-gather.10
  150.5 16.2 all-gather.8
  173.7 24.3 reduce-scatter.10
  201.9 26.3 reduce-scatter.8
where the time goes:
time: 238 us; the launch traced here: 237 us
  waiting for transfers between devices  110 us (46%)
  matrix products  64.9 us (27%)
  local copies, waits for them, and re-layouts  40.7 us (17%)
  between operations  16.3 us (7%)
  other arithmetic  4.58 us (2%)
    all_gather x2, waiting for transfers between devices, apply_operator(): lax.all_gather(vectors, 'col', axis=0, tiled=True)  56 us
    reduce_scatter x2, waiting for transfers between devices, sum_rows(): lax.psum_scatter(row_partial.astype(jnp.bfloat16), 'col', scatter_dimensi...  51.5 us
    dot_general x2, matrix products, row_terms(): jnp.einsum('sij,sjn->sin', hamiltonian, picked, preferred_element_type=jn...  25 us
    dot_general x2, matrix products, col_terms(): jnp.einsum('sji,sjn->sin', hamiltonian, picked, preferred_element_type=jn...  19.6 us
    dot_general x2, local copies, waits for them, and re-layouts, row_terms(): jnp.einsum('sij,sjn->sin', hamiltonian, picked, preferred_element_type=jn...  13.3 us
    dot_general x2, local copies, waits for them, and re-layouts, col_terms(): jnp.einsum('sji,sjn->sin', hamiltonian, picked, preferred_element_type=jn...  13.1 us
    dot_general x2, matrix products, row_terms(): jnp.einsum('rs,sin->rin', row_table, products, precision=lax.Precision.HI...  10.2 us
    dot_general x2, matrix products, col_terms(): jnp.einsum('rs,sin->rin', col_table, products, precision=lax.Precision.HI...  10.1 us
  transfers between devices with their start and end apart: 8, of which 4 were waited for; matrix products, arithmetic and copies ran while one was open for 45% of the time, Pallas kernels for 0%

commit v1 on v0

v1 whole, which is shorter than its diff:
```python
import functools

import jax
import jax.numpy as jnp
from jax import lax
from jax.experimental import pallas as pl
from jax.experimental.pallas import tpu as pltpu
from jax.sharding import PartitionSpec as P

MESH = pl.DeviceIdType.MESH
F32 = jnp.float32
BF16 = jnp.bfloat16
LANES = 128


def kernel(
    n_row, n_col, per, block, width, slots,
    tab, cut, top, v_ref, t_hbm, out1, out2,
    tbuf, prod, colset0, colset1, rowset0, rowset1, rb, rsr0, rsr1, cb, crecv0, crecv1, accr, acct,
    tsem, ag_s, ag_r, xv_s, xv_r, rs_s, rs_r, xc_s, xc_r,
):
    temp = lax.axis_index("temp")
    p = lax.axis_index("row")
    q = lax.axis_index("col")
    row_span = per * n_col
    col_span = per * n_row
    colset = (colset0, colset1)
    rowset = (rowset0, rowset1)
    rsr = (rsr0, rsr1)
    crecv = (crecv0, crecv1)
    row_table = 2 * slots
    col_table = row_table + row_span * col_span
    has_left = q > 0
    has_right = q < n_col - 1

    def tile_copy(t):
        return pltpu.make_async_copy(t_hbm.at[t], tbuf.at[t], tsem.at[t])

    def start_tile(t, carry):
        tile_copy(t).start()
        return carry

    lax.fori_loop(0, slots, start_tile, 0)

    barrier = pltpu.get_barrier_semaphore()
    for s in range(n_row):
        @pl.when(s != p)
        def _():
            pl.semaphore_signal(barrier, inc=1, device_id=(temp, s, q), device_id_type=MESH)

    @pl.when(has_left)
    def _():
        pl.semaphore_signal(barrier, inc=1, device_id=(temp, p, q - 1), device_id_type=MESH)

    @pl.when(has_right)
    def _():
        pl.semaphore_signal(barrier, inc=1, device_id=(temp, p, q + 1), device_id_type=MESH)

    pl.semaphore_wait(barrier, n_row - 1 + has_left.astype(jnp.int32) + has_right.astype(jnp.int32))

    center = (cut[0] + top[0]) * 0.5
    half_width = (top[0] - cut[0]) * 0.5

    def ag_copy(a, direction, b, to):
        return pltpu.make_async_remote_copy(
            src_ref=rowset[a].at[b], dst_ref=rowset[a].at[b],
            send_sem=ag_s.at[a, direction, b], recv_sem=ag_r.at[a, b],
            device_id=(temp, p, to), device_id_type=MESH,
        )

    def xv_copy(a, b, to, h):
        return pltpu.make_async_remote_copy(
            src_ref=colset[a].at[b], dst_ref=colset[a].at[b],
            send_sem=xv_s.at[a, to * per + h], recv_sem=xv_r.at[a, b],
            device_id=(temp, to, q), device_id_type=MESH,
        )

    def rs_copy(a, d, h, slot, to):
        return pltpu.make_async_remote_copy(
            src_ref=rb.at[d * per + h], dst_ref=rsr[a].at[slot * per + h],
            send_sem=rs_s.at[a, d * per + h], recv_sem=rs_r.at[a, slot * per + h],
            device_id=(temp, p, to), device_id_type=MESH,
        )

    def xc_copy(a, d, h, source, to):
        return pltpu.make_async_remote_copy(
            src_ref=cb.at[d * per + h], dst_ref=crecv[a].at[source * per + h],
            send_sem=xc_s.at[a, d * per + h], recv_sem=xc_r.at[a, source * per + h],
            device_id=(temp, to, q), device_id_type=MESH,
        )

    def ag_step(a, k, h):
        low = q - k
        high = q + k

        @pl.when(low >= 0)
        def _():
            b = low * per + h
            if k > 0:
                ag_copy(a, 0, b, q).wait_recv()
            if k < n_col - 1:
                @pl.when(has_right)
                def _():
                    ag_copy(a, 0, b, q + 1).start()

        @pl.when(high < n_col)
        def _():
            b = high * per + h
            if k > 0:
                ag_copy(a, 1, b, q).wait_recv()
            if k < n_col - 1:
                @pl.when(has_left)
                def _():
                    ag_copy(a, 1, b, q - 1).start()

    def send_vectors(a, h, value):
        colset[a][p * per + h] = value
        for s in range(n_row - 1):
            @pl.when(s < p)
            def _():
                xv_copy(a, p * per + h, s, h).start()
        rowset[a][q * per + h] = value.astype(F32).T.astype(BF16)
        ag_step(a, 0, h)

    def row_products(a):
        def one(t, carry):
            if a == 0:
                tile_copy(t).wait()
            prod[t] = jnp.dot(tbuf[t], colset[a][tab[t]], preferred_element_type=F32)
            return carry

        lax.fori_loop(0, slots, one, 0)

        def total(i, carry):
            base = row_table + i * col_span
            ids = [tab[base + c] for c in range(col_span)]
            for m in range(block // LANES):
                rows = pl.ds(m * LANES, LANES)
                acc = prod[ids[0], rows, :]
                for c in range(1, col_span):
                    acc = acc + prod[ids[c], rows, :]
                rb[i, rows, :] = acc.astype(BF16)
            return carry

        lax.fori_loop(0, row_span, total, 0)

    def col_products(a):
        def one(t, carry):
            out = jnp.dot(rowset[a][tab[slots + t]], tbuf[t], preferred_element_type=F32)
            for m in range(block // LANES):
                prod[t, m * width:(m + 1) * width, :] = out[:, m * LANES:(m + 1) * LANES]
            return carry

        lax.fori_loop(0, slots, one, 0)

        def total(c, carry):
            ids = [tab[col_table + r * col_span + c] for r in range(row_span)]
            for m in range(block // LANES):
                rows = pl.ds(m * width, width)
                acc = prod[ids[0], rows, :]
                for r in range(1, row_span):
                    acc = acc + prod[ids[r], rows, :]
                cb[c, :, m * LANES:(m + 1) * LANES] = acc.astype(BF16)
            return carry

        lax.fori_loop(p * per, col_span, total, 0)

    def rs_step(a, tau):
        for h in range(per):
            @pl.when(jnp.logical_and(has_right, tau >= q))
            def _():
                d = n_col - 1 - tau + q

                @pl.when(has_left)
                def _():
                    rs_copy(a, d, h, d + 1, q).wait_recv()
                    mine = rb[d * per + h].astype(F32)
                    rb[d * per + h] = (mine + rsr[a][(d + 1) * per + h].astype(F32)).astype(BF16)

                rs_copy(a, d, h, d + 1, q + 1).start()

            @pl.when(jnp.logical_and(has_left, tau >= n_col - 1 - q))
            def _():
                d = tau - (n_col - 1 - q)

                @pl.when(has_right)
                def _():
                    rs_copy(a, d, h, d, q).wait_recv()
                    mine = rb[d * per + h].astype(F32)
                    rb[d * per + h] = (mine + rsr[a][d * per + h].astype(F32)).astype(BF16)

                rs_copy(a, d, h, d, q - 1).start()

    def wait_rs_sends(a):
        for d in range(n_col):
            @pl.when(d != q)
            def _():
                for h in range(per):
                    rs_copy(a, d, h, d, q).wait_send()

    def wait_xc_sends(a):
        for s in range(1, n_row):
            @pl.when(s > p)
            def _():
                for h in range(per):
                    xc_copy(a, s, h, p, s).wait_send()

    def wait_vector_sends(a):
        for s in range(n_row - 1):
            @pl.when(s < p)
            def _():
                for h in range(per):
                    xv_copy(a, p * per + h, s, h).wait_send()
        for b in range(n_col):
            for h in range(per):
                @pl.when(jnp.logical_and(has_right, b <= q))
                def _():
                    ag_copy(a, 0, b * per + h, q).wait_send()

                @pl.when(jnp.logical_and(has_left, b >= q))
                def _():
                    ag_copy(a, 1, b * per + h, q).wait_send()

    def image(a, h):
        acct[...] = cb[p * per + h].astype(F32)
        for s in range(n_row - 1):
            @pl.when(s < p)
            def _():
                xc_copy(a, p, h, s, p).wait_recv()
                acct[...] += crecv[a][s * per + h].astype(F32)
        accr[...] = rb[q * per + h].astype(F32) + acct[...].T

        @pl.when(has_left)
        def _():
            rs_copy(a, q, h, q + 1, q).wait_recv()
            accr[...] += rsr[a][(q + 1) * per + h].astype(F32)

        @pl.when(has_right)
        def _():
            rs_copy(a, q, h, q, q).wait_recv()
            accr[...] += rsr[a][q * per + h].astype(F32)

        return accr[...]

    def apply(a):
        for k in range(1, n_col - 1):
            for h in range(per):
                ag_step(a, k, h)
        for s in range(1, n_row):
            @pl.when(s > p)
            def _():
                for h in range(per):
                    xv_copy(a, s * per + h, 0, h).wait_recv()
        if a > 0:
            wait_rs_sends(a - 1)
        row_products(a)
        rs_step(a, 0)
        for h in range(per):
            ag_step(a, n_col - 1, h)
        if a > 0:
            wait_xc_sends(a - 1)
        col_products(a)
        for s in range(n_row - 1, 0, -1):
            @pl.when(s > p)
            def _():
                for h in range(per):
                    xc_copy(a, s, h, p, s).start()

        def step(tau, carry):
            rs_step(a, tau)
            return carry

        lax.fori_loop(1, n_col - 1, step, 0)

    prod[slots] = jnp.zeros((block, width), F32)
    for h in range(per):
        send_vectors(0, h, v_ref[h * block:(h + 1) * block, :])
    apply(0)
    for h in range(per):
        rows = pl.ds(h * block, block)
        vectors = v_ref[rows, :].astype(F32)
        first = ((image(0, h) - center * vectors) / half_width).astype(BF16)
        out1[rows, :] = first
        send_vectors(1, h, first)
    apply(1)
    for h in range(per):
        rows = pl.ds(h * block, block)
        vectors = v_ref[rows, :].astype(F32)
        first = out1[rows, :].astype(F32)
        out2[rows, :] = (2.0 * (image(1, h) - center * first) / half_width - vectors).astype(BF16)
    wait_rs_sends(1)
    wait_xc_sends(1)
    wait_vector_sends(0)
    wait_vector_sends(1)


def body(subspace, hamiltonian, tile_blocks, tile_count, cut_bound, top_bound):
    block = hamiltonian.shape[1]
    width = subspace.shape[1]
    slots = hamiltonian.shape[0]
    per = subspace.shape[0] // block
    n_row = lax.axis_size("row")
    n_col = lax.axis_size("col")
    row_span = per * n_col
    col_span = per * n_row
    first = tile_blocks[0, :, 0]
    second = tile_blocks[0, :, 1]
    local_rows = first - lax.axis_index("row") * row_span
    local_cols = second // row_span * per + second % per
    slot_ids = jnp.arange(slots, dtype=jnp.int32)
    live = slot_ids < tile_count[0]
    place = local_rows * col_span + local_cols
    places = jnp.arange(row_span * col_span, dtype=jnp.int32)
    hit = jnp.logical_and(places[:, None] == place[None, :], live[None, :])
    row_slot = jnp.min(jnp.where(hit, slot_ids[None, :], slots), axis=1)
    upper = jnp.logical_and(hit, (first != second)[None, :])
    col_slot = jnp.min(jnp.where(upper, slot_ids[None, :], slots), axis=1)
    tab = jnp.concatenate([local_cols, local_rows, row_slot, col_slot])

    vmem = functools.partial(pl.BlockSpec, memory_space=pltpu.VMEM)
    smem = functools.partial(pl.BlockSpec, memory_space=pltpu.SMEM)
    cols = pltpu.VMEM((col_span, block, width), BF16)
    rows = pltpu.VMEM((row_span, width, block), BF16)
    arrivals = pltpu.VMEM((row_span + per, block, width), BF16)
    col_terms = pltpu.VMEM((col_span, width, block), BF16)
    dma = pltpu.SemaphoreType.DMA
    shape = jax.ShapeDtypeStruct(subspace.shape, BF16)
    return pl.pallas_call(
        functools.partial(kernel, n_row, n_col, per, block, width, slots),
        out_shape=(shape, shape),
        in_specs=[smem(), smem(), smem(), vmem(), pl.BlockSpec(memory_space=pl.ANY)],
        out_specs=(vmem(), vmem()),
        scratch_shapes=[
            pltpu.VMEM((slots, block, block), BF16),
            pltpu.VMEM((slots + 1, block, width), F32),
            cols, cols, rows, rows,
            pltpu.VMEM((row_span, block, width), BF16),
            arrivals, arrivals,
            col_terms, col_terms, col_terms,
            pltpu.VMEM((block, width), F32),
            pltpu.VMEM((width, block), F32),
            dma((slots,)),
            dma((2, 2, row_span)),
            dma((2, row_span)),
            dma((2, col_span)),
            dma((2, col_span)),
            dma((2, row_span)),
            dma((2, row_span + per)),
            dma((2, col_span)),
            dma((2, col_span)),
        ],
        compiler_params=pltpu.CompilerParams(
            collective_id=0, has_side_effects=True, vmem_limit_bytes=60 * 1024 * 1024
        ),
    )(tab, cut_bound, top_bound, subspace, hamiltonian)


def solution(mesh):
    return jax.shard_map(
        body,
        mesh=mesh,
        in_specs=(
            P(("temp", "row", "col"), None),
            P(("temp", "row", "col"), None, None),
            P(("row", "col"), None, None),
            P(("row", "col")),
            P("temp"),
            P("temp"),
        ),
        out_specs=(P(("temp", "row", "col"), None), P(("temp", "row", "col"), None)),
        check_vma=False,
    )
```

time: 238 us -> 95.5 us (0.40)
  waiting for transfers between devices: 110 us -> 0 us
  Pallas kernels: 0 us -> 87 us
  matrix products: 64.9 us -> 0 us
  local copies, waits for them, and re-layouts: 40.7 us -> 3.34 us
  between operations: 16.3 us -> 2.58 us
    pallas_call x0 -> x1, Pallas kernels: none -> 87 us  [body(): pl.pallas_call(functools.partial(kernel, n_row, n_col, per, block, width,...]
    dot_general x8 -> x0, matrix products: 64.9 us -> none  [the longest x2 25 us: row_terms(): jnp.einsum('sij,sjn->sin', hamiltonian, picked, preferred_element_type=jn...]
    all_gather x4 -> x0, waiting for transfers between devices: 56 us -> none  [the longest x2 56 us: apply_operator(): lax.all_gather(vectors, 'col', axis=0, tiled=True)]
    reduce_scatter x4 -> x0, waiting for transfers between devices: 51.6 us -> none  [the longest x2 51.5 us: sum_rows(): lax.psum_scatter(row_partial.astype(jnp.bfloat16), 'col', scatter_dimensi...]
    dot_general x4 -> x0, local copies, waits for them, and re-layouts: 26.5 us -> none  [the longest x2 13.3 us: row_terms(): jnp.einsum('sij,sjn->sin', hamiltonian, picked, preferred_element_type=jn...]
    gather x4 -> x0, local copies, waits for them, and re-layouts: 9.5 us -> none  [the longest x2 4.75 us: row_terms(): picked = jnp.take(column_set, local_cols, axis=0)]
    convert_element_type x4 -> x0, local copies, waits for them, and re-layouts: 4.73 us -> none  [the longest x2 2.43 us: sum_columns(): col_partial.astype(jnp.bfloat16)]
    convert_element_type x2 -> x0, other arithmetic: 3.78 us -> none  [the longest x1 1.9 us: body(): filtered = (2.0 / half_width * (image_two - center * filtered_first.astyp...]
  transfers between devices with their start and end apart: 8 -> 0, of which waited for: 4 -> 0; matrix products, arithmetic and copies ran while one was open for 45% -> 0% of each run, Pallas kernels for 0% -> 0%
where the time goes in v1:
time: 95.5 us; the launch traced here: 95.2 us
  Pallas kernels  87 us (91%)
  local copies, waits for them, and re-layouts  3.34 us (3%)
  between operations  2.58 us (3%)
  other arithmetic  2.27 us (2%)
    pallas_call x1, Pallas kernels, body(): pl.pallas_call(functools.partial(kernel, n_row, n_col, per, block, width,...  87 us
    unnamed x2, local copies, waits for them, and re-layouts  3.34 us

profile of v1, /device:TPU:0, one launch (start us, length us, event | category | flops | bytes accessed | tf_op | source)
XLA Modules:
  0.0 95.2 jit_solution(6311822806500953278)
XLA Ops:
  2.6 0.8 bitcast_compare_fusion
  3.3 0.8 multiply_add_fusion
  4.1 0.1 select_reduce_fusion.1
  4.2 0.6 pad_add_fusion.tab
  4.8 87.0 %shard_map.77 = (bf16[1024,128]{1,0:T(8,128)(2,1)}, bf16[1024,128]{1,0:T(8,128)(2,1)}) custom-call(s32[176]{0:T(256)} %pad_add_fusion.tab, f32[1]{0:T(128)S(6)} %copy.11.cut, f32[1]{0:T(128)S(6)} %copy.12.top, bf16[1024,128]{1,0:T(8,128)(2,1)} %v_ref.1, bf16[24,512,512]{2,1,0:T(8,128)(2,1)} %t_hbm.1), custom_call_target="tpu_custom_call" | custom-call | tf_op jit(solution)/shard_map/pallas_call | solution.py:328
  91.9 1.7 %copy.13 = bf16[1024,128]{1,0:T(8,128)(2,1)} copy(bf16[1024,128]{1,0:T(8,128)(2,1)} %get-tuple-element.11) | data formatting | bytes 524288
  93.5 1.7 %copy.14 = bf16[1024,128]{1,0:T(8,128)(2,1)} copy(bf16[1024,128]{1,0:T(8,128)(2,1)} %get-tuple-element.12) | data formatting | bytes 524288

commit v2 on v1

--- a/solution.py
+++ b/solution.py
@@ -11,13 +11,14 @@
 F32 = jnp.float32
 BF16 = jnp.bfloat16
 LANES = 128
+UNROLL = 4
 
 
 def kernel(
     n_row, n_col, per, block, width, slots,
-    tab, cut, top, v_ref, t_hbm, out1, out2,
+    pairs, count, cut, top, v_ref, t_hbm, out1, out2,
     tbuf, prod, colset0, colset1, rowset0, rowset1, rb, rsr0, rsr1, cb, crecv0, crecv1, accr, acct,
-    tsem, ag_s, ag_r, xv_s, xv_r, rs_s, rs_r, xc_s, xc_r,
+    keys, vec_slot, row_slot, col_slot, tsem, ag_s, ag_r, xv_s, xv_r, rs_s, rs_r, xc_s, xc_r,
 ):
     temp = lax.axis_index("temp")
     p = lax.axis_index("row")
@@ -28,8 +29,10 @@
     rowset = (rowset0, rowset1)
     rsr = (rsr0, rsr1)
     crecv = (crecv0, crecv1)
-    row_table = 2 * slots
-    col_table = row_table + row_span * col_span
+    core = lax.rem(p, 2)
+    chip = p // 2
+    sib = p + 1 - 2 * core
+    chips = n_row // 2
     has_left = q > 0
     has_right = q < n_col - 1
 
@@ -113,27 +116,96 @@
                 def _():
                     ag_copy(a, 1, b, q - 1).start()
 
+    def later_chips(fn):
+        for x in range(1, chips):
+            @pl.when(x > chip)
+            def _():
+                fn(x)
+
+    def earlier_chips(fn):
+        for x in range(chips - 1):
+            @pl.when(x < chip)
+            def _():
+                fn(x)
+
     def send_vectors(a, h, value):
-        colset[a][p * per + h] = value
-        for s in range(n_row - 1):
-            @pl.when(s < p)
-            def _():
-                xv_copy(a, p * per + h, s, h).start()
+        mine = p * per + h
+        colset[a][mine] = value
+        earlier_chips(lambda x: xv_copy(a, mine, 2 * x + core, h).start())
+
+        @pl.when(core == 1)
+        def _():
+            xv_copy(a, mine, sib, h).start()
+
         rowset[a][q * per + h] = value.astype(F32).T.astype(BF16)
         ag_step(a, 0, h)
 
-    def row_products(a):
-        def one(t, carry):
+    def forward_copy(a, x, h):
+        s = 2 * x + core
+        return pltpu.make_async_remote_copy(
+            src_ref=colset[a].at[s * per + h], dst_ref=colset[a].at[s * per + h],
+            send_sem=xv_s.at[a, s * per + h], recv_sem=xv_r.at[a, s * per + h],
+            device_id=(temp, sib, q), device_id_type=MESH,
+        )
+
+    def finish_row_gather(a):
+        for h in range(per):
+            def relay(x):
+                xv_copy(a, (2 * x + core) * per + h, sib, h).wait_recv()
+                forward_copy(a, x, h).start()
+
+            later_chips(relay)
+        for h in range(per):
+            @pl.when(core == 0)
+            def _():
+                xv_copy(a, sib * per + h, sib, h).wait_recv()
+
+            later_chips(lambda x: xv_copy(a, (2 * x + 1 - core) * per + h, sib, h).wait_recv())
+
+    def find_slots():
+        for t in range(slots):
+            first = pairs[0, t, 0]
+            second = pairs[0, t, 1]
+            local_row = first - p * row_span
+            local_col = second // row_span * per + lax.rem(second, per)
+            vec_slot[t] = jnp.clip(local_col, 0, col_span - 1)
+            vec_slot[slots + t] = jnp.clip(local_row, 0, row_span - 1)
+            keys[t] = jnp.where(t < count[0], local_row * col_span + local_col, -1)
+        held = [keys[t] for t in range(slots)]
+
+        def find(i, carry):
+            slot = jnp.int32(slots)
+            for t in range(slots):
+                slot = jnp.where(held[t] == i, t, slot)
+            row_slot[i] = slot
+            col_slot[i] = slot
+            return carry
+
+        lax.fori_loop(0, row_span * col_span, find, 0)
+        for k in range(per):
+            col_slot[(q * per + k) * col_span + p * per + k] = slots
+
+    def grouped(lo, hi, one):
+        group = UNROLL if (hi - lo) % UNROLL == 0 else 1
+
+        def several(g, carry):
+            for u in range(group):
+                one(lo + g * group + u)
+            return carry
+
+        lax.fori_loop(0, (hi - lo) // group, several, 0)
+
+    def row_products(a, lo, hi):
+        def one(t):
             if a == 0:
                 tile_copy(t).wait()
-            prod[t] = jnp.dot(tbuf[t], colset[a][tab[t]], preferred_element_type=F32)
-            return carry
-
-        lax.fori_loop(0, slots, one, 0)
-
+            prod[t] = jnp.dot(tbuf[t], colset[a][vec_slot[t]], preferred_element_type=F32)
+
+        grouped(lo, hi, one)
+
+    def row_totals():
         def total(i, carry):
-            base = row_table + i * col_span
-            ids = [tab[base + c] for c in range(col_span)]
+            ids = [row_slot[i * col_span + c] for c in range(col_span)]
             for m in range(block // LANES):
                 rows = pl.ds(m * LANES, LANES)
                 acc = prod[ids[0], rows, :]
@@ -145,16 +217,16 @@
         lax.fori_loop(0, row_span, total, 0)
 
     def col_products(a):
-        def one(t, carry):
-            out = jnp.dot(rowset[a][tab[slots + t]], tbuf[t], preferred_element_type=F32)
+        def one(t):
+            out = jnp.dot(rowset[a][vec_slot[slots + t]], tbuf[t], preferred_element_type=F32)
             for m in range(block // LANES):
                 prod[t, m * width:(m + 1) * width, :] = out[:, m * LANES:(m + 1) * LANES]
-            return carry
-
-        lax.fori_loop(0, slots, one, 0)
-
+
+        grouped(0, slots, one)
+
+    def col_totals():
         def total(c, carry):
-            ids = [tab[col_table + r * col_span + c] for r in range(row_span)]
+            ids = [col_slot[r * col_span + c] for r in range(row_span)]
             for m in range(block // LANES):
                 rows = pl.ds(m * width, width)
                 acc = prod[ids[0], rows, :]
@@ -165,6 +237,29 @@
 
         lax.fori_loop(p * per, col_span, total, 0)
 
+    def send_col_sums(a):
+        @pl.when(core == 0)
+        def _():
+            for h in range(per):
+                xc_copy(a, sib, h, chip, sib).start()
+
+        def to_sibling(x):
+            d = 2 * x + 1 - core
+            for h in range(per):
+                xc_copy(a, d, h, d, sib).start()
+
+        later_chips(to_sibling)
+
+        def across(x):
+            d = 2 * x + core
+            for h in range(per):
+                xc_copy(a, d, h, d, sib).wait_recv()
+                mine = cb[d * per + h].astype(F32)
+                cb[d * per + h] = (mine + crecv[a][d * per + h].astype(F32)).astype(BF16)
+                xc_copy(a, d, h, chip, d).start()
+
+        later_chips(across)
+
     def rs_step(a, tau):
         for h in range(per):
             @pl.when(jnp.logical_and(has_right, tau >= q))
@@ -206,11 +301,14 @@
                     xc_copy(a, s, h, p, s).wait_send()
 
     def wait_vector_sends(a):
-        for s in range(n_row - 1):
-            @pl.when(s < p)
-            def _():
-                for h in range(per):
-                    xv_copy(a, p * per + h, s, h).wait_send()
+        for h in range(per):
+            earlier_chips(lambda x: xv_copy(a, p * per + h, 2 * x + core, h).wait_send())
+
+            @pl.when(core == 1)
+            def _():
+                xv_copy(a, p * per + h, sib, h).wait_send()
+
+            later_chips(lambda x: forward_copy(a, x, h).wait_send())
         for b in range(n_col):
             for h in range(per):
                 @pl.when(jnp.logical_and(has_right, b <= q))
@@ -223,11 +321,16 @@
 
     def image(a, h):
         acct[...] = cb[p * per + h].astype(F32)
-        for s in range(n_row - 1):
-            @pl.when(s < p)
-            def _():
-                xc_copy(a, p, h, s, p).wait_recv()
-                acct[...] += crecv[a][s * per + h].astype(F32)
+
+        def add(x):
+            xc_copy(a, p, h, x, p).wait_recv()
+            acct[...] += crecv[a][x * per + h].astype(F32)
+
+        @pl.when(core == 1)
+        def _():
+            add(chip)
+
+        earlier_chips(add)
         accr[...] = rb[q * per + h].astype(F32) + acct[...].T
 
         @pl.when(has_left)
@@ -243,38 +346,37 @@
         return accr[...]
 
     def apply(a):
-        for k in range(1, n_col - 1):
+        for h in range(per):
+            ag_step(a, 1, h)
+        finish_row_gather(a)
+        row_products(a, 0, slots // 2)
+        for k in range(2, n_col - 1):
             for h in range(per):
                 ag_step(a, k, h)
-        for s in range(1, n_row):
-            @pl.when(s > p)
-            def _():
-                for h in range(per):
-                    xv_copy(a, s * per + h, 0, h).wait_recv()
+        row_products(a, slots // 2, slots)
         if a > 0:
             wait_rs_sends(a - 1)
-        row_products(a)
+        row_totals()
         rs_step(a, 0)
         for h in range(per):
             ag_step(a, n_col - 1, h)
         if a > 0:
             wait_xc_sends(a - 1)
+        rs_step(a, 1)
         col_products(a)
-        for s in range(n_row - 1, 0, -1):
-            @pl.when(s > p)
-            def _():
-                for h in range(per):
-                    xc_copy(a, s, h, p, s).start()
+        col_totals()
+        send_col_sums(a)
 
         def step(tau, carry):
             rs_step(a, tau)
             return carry
 
-        lax.fori_loop(1, n_col - 1, step, 0)
+        lax.fori_loop(2, n_col - 1, step, 0)
 
     prod[slots] = jnp.zeros((block, width), F32)
     for h in range(per):
         send_vectors(0, h, v_ref[h * block:(h + 1) * block, :])
+    find_slots()
     apply(0)
     for h in range(per):
         rows = pl.ds(h * block, block)
@@ -303,20 +405,6 @@
     n_col = lax.axis_size("col")
     row_span = per * n_col
     col_span = per * n_row
-    first = tile_blocks[0, :, 0]
-    second = tile_blocks[0, :, 1]
-    local_rows = first - lax.axis_index("row") * row_span
-    local_cols = second // row_span * per + second % per
-    slot_ids = jnp.arange(slots, dtype=jnp.int32)
-    live = slot_ids < tile_count[0]
-    place = local_rows * col_span + local_cols
-    places = jnp.arange(row_span * col_span, dtype=jnp.int32)
-    hit = jnp.logical_and(places[:, None] == place[None, :], live[None, :])
-    row_slot = jnp.min(jnp.where(hit, slot_ids[None, :], slots), axis=1)
-    upper = jnp.logical_and(hit, (first != second)[None, :])
-    col_slot = jnp.min(jnp.where(upper, slot_ids[None, :], slots), axis=1)
-    tab = jnp.concatenate([local_cols, local_rows, row_slot, col_slot])
-
     vmem = functools.partial(pl.BlockSpec, memory_space=pltpu.VMEM)
     smem = functools.partial(pl.BlockSpec, memory_space=pltpu.SMEM)
     cols = pltpu.VMEM((col_span, block, width), BF16)
@@ -328,7 +416,7 @@
     return pl.pallas_call(
         functools.partial(kernel, n_row, n_col, per, block, width, slots),
         out_shape=(shape, shape),
-        in_specs=[smem(), smem(), smem(), vmem(), pl.BlockSpec(memory_space=pl.ANY)],
+        in_specs=[smem(), smem(), smem(), smem(), vmem(), pl.BlockSpec(memory_space=pl.ANY)],
         out_specs=(vmem(), vmem()),
         scratch_shapes=[
             pltpu.VMEM((slots, block, block), BF16),
@@ -339,6 +427,10 @@
             col_terms, col_terms, col_terms,
             pltpu.VMEM((block, width), F32),
             pltpu.VMEM((width, block), F32),
+            pltpu.SMEM((slots,), jnp.int32),
+            pltpu.SMEM((2 * slots,), jnp.int32),
+            pltpu.SMEM((row_span * col_span,), jnp.int32),
+            pltpu.SMEM((row_span * col_span,), jnp.int32),
             dma((slots,)),
             dma((2, 2, row_span)),
             dma((2, row_span)),
@@ -352,7 +444,7 @@
         compiler_params=pltpu.CompilerParams(
             collective_id=0, has_side_effects=True, vmem_limit_bytes=60 * 1024 * 1024
         ),
-    )(tab, cut_bound, top_bound, subspace, hamiltonian)
+    )(tile_blocks, tile_count, cut_bound, top_bound, subspace, hamiltonian)
 
 
 def solution(mesh):

time: 95.5 us -> 88 us (0.921)
  Pallas kernels: 87 us -> 80.2 us
  other arithmetic: 2.27 us -> 0 us
  local copies, waits for them, and re-layouts: 3.34 us -> 4.7 us
    pallas_call x1, Pallas kernels: 87 us -> 80.2 us  [body(): pl.pallas_call(functools.partial(kernel, n_row, n_col, per, block, width,...]
    unnamed x2 -> x3, local copies, waits for them, and re-layouts: 3.34 us -> 4.7 us
where the time goes in v2:
time: 88 us; the launch traced here: 87.5 us
  Pallas kernels  80.2 us (91%)
  local copies, waits for them, and re-layouts  4.7 us (5%)
  between operations  2.58 us (3%)
    pallas_call x1, Pallas kernels, body(): pl.pallas_call(functools.partial(kernel, n_row, n_col, per, block, width,...  80.2 us
    unnamed x3, local copies, waits for them, and re-layouts  4.7 us

profile of v2, /device:TPU:0, one launch (start us, length us, event | category | flops | bytes accessed | tf_op | source)
XLA Modules:
  0.0 87.5 jit_solution(2724997198516837844)
XLA Ops:
  2.6 1.4 %copy.8.pairs = s32[1,24,2]{2,1,0:T(8,128)} copy(s32[1,24,2]{1,2,0:T(2,128)} %param.8) | data formatting | bytes 384 | tf_op args[2]
  3.9 80.2 %shard_map.77 = (bf16[1024,128]{1,0:T(8,128)(2,1)}, bf16[1024,128]{1,0:T(8,128)(2,1)}) custom-call(s32[1,24,2]{2,1,0:T(8,128)} %copy.8.pairs, s32[1]{0:T(128)S(6)} %copy.11.count, f32[1]{0:T(128)S(6)} %copy.12.cut, f32[1]{0:T(128)S(6)} %copy.13.top, bf16[1024,128]{1,0:T(8,128)(2,1)} %v_ref.1, bf16[24,512,512]{2,1,0:T(8,128)(2,1)} %t_hbm.1), custom_call_target="tpu_custom_call" | custom-call | tf_op jit(solution)/shard_map/pallas_call | solution.py:416
  84.1 1.7 %copy.14 = bf16[1024,128]{1,0:T(8,128)(2,1)} copy(bf16[1024,128]{1,0:T(8,128)(2,1)} %get-tuple-element.4) | data formatting | bytes 524288
  85.8 1.7 %copy.15 = bf16[1024,128]{1,0:T(8,128)(2,1)} copy(bf16[1024,128]{1,0:T(8,128)(2,1)} %get-tuple-element.5) | data formatting | bytes 524288

commit v3 on v2

v3 whole, which is shorter than its diff:
```python
import functools

import jax
import jax.numpy as jnp
from jax import lax
from jax.experimental import pallas as pl
from jax.experimental.pallas import tpu as pltpu
from jax.sharding import PartitionSpec as P

MESH = pl.DeviceIdType.MESH
F32 = jnp.float32
BF16 = jnp.bfloat16
PIECE = 32
UNROLL = 8
HALVES = 2


def kernel(
    n_row, n_col, per, block, width, slots, turned,
    pairs, count, cut, top, v_ref, t_hbm, out1, out2,
    tbuf, tbuf_t, prod, col00, col01, col10, col11, row00, row01, row10, row11, rb, rsr0, rsr1, cb, crecv0, crecv1, acc, held32, wide,
    keys, vec_slot, row_slot, col_slot, tsem, ag_s, ag_r, xv_s, xv_r, rs_s, rs_r, xc_s, xc_r,
):
    temp = lax.axis_index("temp")
    p = lax.axis_index("row")
    q = lax.axis_index("col")
    row_span = per * n_col
    col_span = per * n_row
    colset = ((col00, col01), (col10, col11))
    rowset = ((row00, row01), (row10, row11))
    half = width // HALVES
    parts = range(HALVES)

    def span(owner):
        return pl.ds(owner * per, per)

    def lines(h):
        return pl.ds(h * half, half)

    rsr = (rsr0, rsr1)
    crecv = (crecv0, crecv1)
    core = lax.rem(p, 2)
    chip = p // 2
    sib = p + 1 - 2 * core
    chips = n_row // 2
    has_left = q > 0
    has_right = q < n_col - 1

    def tile_copy(t):
        return pltpu.make_async_copy(t_hbm.at[t], tbuf.at[t], tsem.at[t])

    def start_tile(t, carry):
        tile_copy(t).start()
        return carry

    lax.fori_loop(0, slots, start_tile, 0)

    barrier = pltpu.get_barrier_semaphore()
    for s in range(n_row):
        @pl.when(s != p)
        def _():
            pl.semaphore_signal(barrier, inc=1, device_id=(temp, s, q), device_id_type=MESH)

    @pl.when(has_left)
    def _():
        pl.semaphore_signal(barrier, inc=1, device_id=(temp, p, q - 1), device_id_type=MESH)

    @pl.when(has_right)
    def _():
        pl.semaphore_signal(barrier, inc=1, device_id=(temp, p, q + 1), device_id_type=MESH)

    pl.semaphore_wait(barrier, n_row - 1 + has_left.astype(jnp.int32) + has_right.astype(jnp.int32))

    center = (cut[0] + top[0]) * 0.5
    half_width = (top[0] - cut[0]) * 0.5

    def ag_copy(a, direction, owner, h, to):
        ref = rowset[a][h].at[span(owner)]
        return pltpu.make_async_remote_copy(
            src_ref=ref, dst_ref=ref,
            send_sem=ag_s.at[a, direction, owner * HALVES + h],
            recv_sem=ag_r.at[a, owner * HALVES + h],
            device_id=(temp, p, to), device_id_type=MESH,
        )

    def xv_copy(a, owner, to, h, send):
        ref = colset[a][h].at[span(owner)]
        return pltpu.make_async_remote_copy(
            src_ref=ref, dst_ref=ref,
            send_sem=xv_s.at[a, send * HALVES + h], recv_sem=xv_r.at[a, owner * HALVES + h],
            device_id=(temp, to, q), device_id_type=MESH,
        )

    def rs_copy(a, d, h, slot, to):
        return pltpu.make_async_remote_copy(
            src_ref=rb.at[span(d), lines(h)], dst_ref=rsr[a].at[span(slot), lines(h)],
            send_sem=rs_s.at[a, d * HALVES + h], recv_sem=rs_r.at[a, slot * HALVES + h],
            device_id=(temp, p, to), device_id_type=MESH,
        )

    def xc_copy(a, d, h, source, to):
        return pltpu.make_async_remote_copy(
            src_ref=cb.at[span(d), lines(h)], dst_ref=crecv[a].at[span(source), lines(h)],
            send_sem=xc_s.at[a, d * HALVES + h], recv_sem=xc_r.at[a, source * HALVES + h],
            device_id=(temp, to, q), device_id_type=MESH,
        )

    def ag_step(a, k, h):
        low = q - k
        high = q + k

        @pl.when(low >= 0)
        def _():
            if k > 0:
                ag_copy(a, 0, low, h, q).wait_recv()
            if k < n_col - 1:
                @pl.when(has_right)
                def _():
                    ag_copy(a, 0, low, h, q + 1).start()

        @pl.when(high < n_col)
        def _():
            if k > 0:
                ag_copy(a, 1, high, h, q).wait_recv()
            if k < n_col - 1:
                @pl.when(has_left)
                def _():
                    ag_copy(a, 1, high, h, q - 1).start()

    def later_chips(fn):
        for x in range(1, chips):
            @pl.when(x > chip)
            def _():
                fn(x)

    def earlier_chips(fn):
        for x in range(chips - 1):
            @pl.when(x < chip)
            def _():
                fn(x)

    def send_vectors(a, h, value):
        colset[a][h][span(p)] = value
        earlier_chips(lambda x: xv_copy(a, p, 2 * x + core, h, 2 * x + core).start())

        @pl.when(core == 1)
        def _():
            xv_copy(a, p, sib, h, sib).start()

        rowset[a][h][span(q)] = value
        ag_step(a, 0, h)

    def forward_copy(a, x, h):
        return xv_copy(a, 2 * x + core, sib, h, 2 * x + core)

    def finish_row_gather(a, h):
        def relay(x):
            forward_copy(a, x, h).wait_recv()
            forward_copy(a, x, h).start()

        later_chips(relay)

        @pl.when(core == 0)
        def _():
            xv_copy(a, sib, sib, h, sib).wait_recv()

        later_chips(lambda x: xv_copy(a, 2 * x + 1 - core, sib, h, sib).wait_recv())

    def find_slots():
        for t in range(slots):
            first = pairs[0, t, 0]
            second = pairs[0, t, 1]
            local_row = first - p * row_span
            local_col = second // row_span * per + lax.rem(second, per)
            vec_slot[t] = jnp.clip(local_col, 0, col_span - 1)
            vec_slot[slots + t] = jnp.clip(local_row, 0, row_span - 1)
            keys[t] = jnp.where(t < count[0], local_row * col_span + local_col, -1)
        held = [keys[t] for t in range(slots)]

        def find(i, carry):
            slot = jnp.int32(slots)
            for t in range(slots):
                slot = jnp.where(held[t] == i, t, slot)
            row_slot[i] = slot
            col_slot[i] = slot
            return carry

        lax.fori_loop(0, row_span * col_span, find, 0)
        for k in range(per):
            col_slot[(q * per + k) * col_span + p * per + k] = slots

    def grouped(lo, hi, one):
        group = UNROLL if (hi - lo) % UNROLL == 0 else 1

        def several(g, carry):
            for u in range(group):
                one(lo + g * group + u)
            return carry

        lax.fori_loop(0, (hi - lo) // group, several, 0)

    def transpose_tiles():
        def one(t, carry):
            tile_copy(t).wait()
            if turned:
                tbuf_t[t] = tbuf[t].T
            return carry

        lax.fori_loop(0, slots, one, 0)

    def row_products(a, h):
        def one(t):
            vectors = colset[a][h][vec_slot[t]]
            if turned:
                prod[t, lines(h), :] = jnp.dot(vectors, tbuf_t[t], preferred_element_type=F32)
            else:
                prod[t, lines(h), :] = lax.dot_general(
                    vectors, tbuf[t], (((1,), (1,)), ((), ())), preferred_element_type=F32
                )

        grouped(0, slots, one)

    def row_totals(h):
        def total(i, carry):
            ids = [row_slot[i * col_span + c] for c in range(col_span)]
            for m in range(half // PIECE):
                rows = pl.ds(h * half + m * PIECE, PIECE)
                acc = prod[ids[0], rows, :]
                for c in range(1, col_span):
                    acc = acc + prod[ids[c], rows, :]
                rb[i, rows, :] = acc.astype(BF16)
            return carry

        lax.fori_loop(0, row_span, total, 0)

    def col_products(a, h):
        def one(t):
            prod[t, lines(h), :] = jnp.dot(
                rowset[a][h][vec_slot[slots + t]], tbuf[t], preferred_element_type=F32
            )

        grouped(0, slots, one)

    def col_totals(h):
        def total(c, carry):
            ids = [col_slot[r * col_span + c] for r in range(row_span)]
            for m in range(half // PIECE):
                rows = pl.ds(h * half + m * PIECE, PIECE)
                acc = prod[ids[0], rows, :]
                for r in range(1, row_span):
                    acc = acc + prod[ids[r], rows, :]
                cb[c, rows, :] = acc.astype(BF16)
            return carry

        lax.fori_loop(p * per, col_span, total, 0)

    def send_to_sibling(a, h):
        @pl.when(core == 0)
        def _():
            xc_copy(a, sib, h, chip, sib).start()

        def to_sibling(x):
            d = 2 * x + 1 - core
            xc_copy(a, d, h, d, sib).start()

        later_chips(to_sibling)

    def send_across(a, h):
        def across(x):
            d = 2 * x + core
            xc_copy(a, d, h, d, sib).wait_recv()
            mine = cb[span(d), lines(h), :].astype(F32)
            cb[span(d), lines(h), :] = (mine + crecv[a][span(d), lines(h), :].astype(F32)).astype(BF16)
            xc_copy(a, d, h, chip, d).start()

        later_chips(across)

    def add_arrival(a, d, h, slot):
        rs_copy(a, d, h, slot, q).wait_recv()
        mine = rb[span(d), lines(h), :].astype(F32)
        rb[span(d), lines(h), :] = (mine + rsr[a][span(slot), lines(h), :].astype(F32)).astype(BF16)

    def rs_step(a, tau, h):
        @pl.when(jnp.logical_and(has_right, tau >= q))
        def _():
            d = n_col - 1 - tau + q

            @pl.when(has_left)
            def _():
                add_arrival(a, d, h, d + 1)

            rs_copy(a, d, h, d + 1, q + 1).start()

        @pl.when(jnp.logical_and(has_left, tau >= n_col - 1 - q))
        def _():
            d = tau - (n_col - 1 - q)

            @pl.when(has_right)
            def _():
                add_arrival(a, d, h, d)

            rs_copy(a, d, h, d, q - 1).start()

    def wait_rs_sends(a):
        for d in range(n_col):
            @pl.when(d != q)
            def _():
                for h in parts:
                    rs_copy(a, d, h, d, q).wait_send()

    def wait_xc_sends(a):
        for s in range(1, n_row):
            @pl.when(s > p)
            def _():
                for h in parts:
                    xc_copy(a, s, h, p, s).wait_send()

    def wait_vector_sends(a):
        for h in parts:
            earlier_chips(lambda x: xv_copy(a, p, 2 * x + core, h, 2 * x + core).wait_send())

            @pl.when(core == 1)
            def _():
                xv_copy(a, p, sib, h, sib).wait_send()

            later_chips(lambda x: forward_copy(a, x, h).wait_send())
            for b in range(n_col):
                @pl.when(jnp.logical_and(has_right, b <= q))
                def _():
                    ag_copy(a, 0, b, h, q).wait_send()

                @pl.when(jnp.logical_and(has_left, b >= q))
                def _():
                    ag_copy(a, 1, b, h, q).wait_send()

    def image(a, h):
        acc[...] = cb[span(p), lines(h), :].astype(F32) + rb[span(q), lines(h), :].astype(F32)

        def add(x):
            xc_copy(a, p, h, x, p).wait_recv()
            acc[...] += crecv[a][span(x), lines(h), :].astype(F32)

        @pl.when(core == 1)
        def _():
            add(chip)

        earlier_chips(add)

        @pl.when(has_left)
        def _():
            rs_copy(a, q, h, q + 1, q).wait_recv()
            acc[...] += rsr[a][span(q + 1), lines(h), :].astype(F32)

        @pl.when(has_right)
        def _():
            rs_copy(a, q, h, q, q).wait_recv()
            acc[...] += rsr[a][span(q), lines(h), :].astype(F32)

        return acc[...]

    def apply(a):
        if a == 0:
            transpose_tiles()
        else:
            wait_rs_sends(a - 1)
        for h in parts:
            ag_step(a, 1, h)
            finish_row_gather(a, h)
            row_products(a, h)
            row_totals(h)
            rs_step(a, 0, h)
        for h in parts:
            for k in range(2, n_col - 1):
                ag_step(a, k, h)
            rs_step(a, 1, h)
        if a > 0:
            wait_xc_sends(a - 1)
        for h in parts:
            ag_step(a, n_col - 1, h)
            col_products(a, h)
            col_totals(h)
            send_to_sibling(a, h)
        for h in parts:
            rs_step(a, 2, h)
            send_across(a, h)

        def step(tau, carry):
            for h in parts:
                rs_step(a, tau, h)
            return carry

        lax.fori_loop(3, n_col - 1, step, 0)

    prod[slots] = jnp.zeros((width, block), F32)
    for k in range(per):
        held32[k] = v_ref[k * block:(k + 1) * block, :].astype(F32).T
    for h in parts:
        send_vectors(0, h, held32[:, lines(h), :].astype(BF16))
    find_slots()
    apply(0)
    for h in parts:
        vectors = held32[:, lines(h), :]
        send_vectors(1, h, ((image(0, h) - center * vectors) / half_width).astype(BF16))
    for k in range(per):
        for h in parts:
            wide[lines(h), :] = colset[1][h][p * per + k].astype(F32)
        out1[k * block:(k + 1) * block, :] = wide[...].T.astype(BF16)
    apply(1)
    for h in parts:
        first = colset[1][h][span(p)].astype(F32)
        vectors = held32[:, lines(h), :]
        held32[:, lines(h), :] = 2.0 * (image(1, h) - center * first) / half_width - vectors
    for k in range(per):
        out2[k * block:(k + 1) * block, :] = held32[k].T.astype(BF16)
    wait_rs_sends(1)
    wait_xc_sends(1)
    wait_vector_sends(0)
    wait_vector_sends(1)


def body(subspace, hamiltonian, tile_blocks, tile_count, cut_bound, top_bound):
    block = hamiltonian.shape[1]
    width = subspace.shape[1]
    slots = hamiltonian.shape[0]
    per = subspace.shape[0] // block
    n_row = lax.axis_size("row")
    n_col = lax.axis_size("col")
    row_span = per * n_col
    col_span = per * n_row
    turned = row_span + col_span <= slots
    vmem = functools.partial(pl.BlockSpec, memory_space=pltpu.VMEM)
    smem = functools.partial(pl.BlockSpec, memory_space=pltpu.SMEM)
    half = width // HALVES
    cols = pltpu.VMEM((col_span, width, block), BF16)
    rows = pltpu.VMEM((row_span, width, block), BF16)
    col_half = pltpu.VMEM((col_span, half, block), BF16)
    row_half = pltpu.VMEM((row_span, half, block), BF16)
    arrivals = pltpu.VMEM((row_span + per, width, block), BF16)
    dma = pltpu.SemaphoreType.DMA
    shape = jax.ShapeDtypeStruct(subspace.shape, BF16)
    return pl.pallas_call(
        functools.partial(kernel, n_row, n_col, per, block, width, slots, turned),
        out_shape=(shape, shape),
        in_specs=[smem(), smem(), smem(), smem(), vmem(), pl.BlockSpec(memory_space=pl.ANY)],
        out_specs=(vmem(), vmem()),
        scratch_shapes=[
            pltpu.VMEM((slots, block, block), BF16),
            pltpu.VMEM((slots if turned else 1, block, block), BF16),
            pltpu.VMEM((slots + 1, width, block), F32),
            col_half, col_half, col_half, col_half,
            row_half, row_half, row_half, row_half,
            rows,
            arrivals, arrivals,
            cols, cols, cols,
            pltpu.VMEM((per, half, block), F32),
            pltpu.VMEM((per, width, block), F32),
            pltpu.VMEM((width, block), F32),
            pltpu.SMEM((slots,), jnp.int32),
            pltpu.SMEM((2 * slots,), jnp.int32),
            pltpu.SMEM((row_span * col_span,), jnp.int32),
            pltpu.SMEM((row_span * col_span,), jnp.int32),
            dma((slots,)),
            dma((2, 2, n_col * HALVES)),
            dma((2, n_col * HALVES)),
            dma((2, n_row * HALVES)),
            dma((2, n_row * HALVES)),
            dma((2, n_col * HALVES)),
            dma((2, (n_col + 1) * HALVES)),
            dma((2, n_row * HALVES)),
            dma((2, n_row * HALVES)),
        ],
        compiler_params=pltpu.CompilerParams(
            collective_id=0, has_side_effects=True, vmem_limit_bytes=60 * 1024 * 1024
        ),
    )(tile_blocks, tile_count, cut_bound, top_bound, subspace, hamiltonian)


def solution(mesh):
    return jax.shard_map(
        body,
        mesh=mesh,
        in_specs=(
            P(("temp", "row", "col"), None),
            P(("temp", "row", "col"), None, None),
            P(("row", "col"), None, None),
            P(("row", "col")),
            P("temp"),
            P("temp"),
        ),
        out_specs=(P(("temp", "row", "col"), None), P(("temp", "row", "col"), None)),
        check_vma=False,
    )
```

time: 88 us -> 79.3 us (0.901)
  Pallas kernels: 80.2 us -> 71.8 us
    pallas_call x1, Pallas kernels: 80.2 us -> 71.8 us  [body(): pl.pallas_call(functools.partial(kernel, n_row, n_col, per, block, width,...]
where the time goes in v3:
time: 79.3 us; the launch traced here: 79 us
  Pallas kernels  71.8 us (91%)
  local copies, waits for them, and re-layouts  4.7 us (6%)
  between operations  2.58 us (3%)
    pallas_call x1, Pallas kernels, body(): pl.pallas_call(functools.partial(kernel, n_row, n_col, per, block, width,...  71.8 us
    unnamed x3, local copies, waits for them, and re-layouts  4.7 us

profile of v3, /device:TPU:0, one launch (start us, length us, event | category | flops | bytes accessed | tf_op | source)
XLA Modules:
  0.0 79.0 jit_solution(5381101261521129857)
XLA Ops:
  2.6 1.4 %copy.8.pairs = s32[1,24,2]{2,1,0:T(8,128)} copy(s32[1,24,2]{1,2,0:T(2,128)} %param.8) | data formatting | bytes 384 | tf_op args[2]
  3.9 71.8 %shard_map.77 = (bf16[1024,128]{1,0:T(8,128)(2,1)}, bf16[1024,128]{1,0:T(8,128)(2,1)}) custom-call(s32[1,24,2]{2,1,0:T(8,128)} %copy.8.pairs, s32[1]{0:T(128)S(6)} %copy.11.count, f32[1]{0:T(128)S(6)} %copy.12.cut, f32[1]{0:T(128)S(6)} %copy.13.top, bf16[1024,128]{1,0:T(8,128)(2,1)} %v_ref.1, bf16[24,512,512]{2,1,0:T(8,128)(2,1)} %t_hbm.1), custom_call_target="tpu_custom_call" | custom-call | tf_op jit(solution)/shard_map/pallas_call | solution.py:441
  75.7 1.7 %copy.14 = bf16[1024,128]{1,0:T(8,128)(2,1)} copy(bf16[1024,128]{1,0:T(8,128)(2,1)} %get-tuple-element.4) | data formatting | bytes 524288
  77.4 1.7 %copy.15 = bf16[1024,128]{1,0:T(8,128)(2,1)} copy(bf16[1024,128]{1,0:T(8,128)(2,1)} %get-tuple-element.5) | data formatting | bytes 524288

commit v4 on v3

--- a/solution.py
+++ b/solution.py
@@ -364,8 +364,8 @@
         else:
             wait_rs_sends(a - 1)
         for h in parts:
+            finish_row_gather(a, h)
             ag_step(a, 1, h)
-            finish_row_gather(a, h)
             row_products(a, h)
             row_totals(h)
             rs_step(a, 0, h)
@@ -380,7 +380,6 @@
             col_products(a, h)
             col_totals(h)
             send_to_sibling(a, h)
-        for h in parts:
             rs_step(a, 2, h)
             send_across(a, h)
 

time: 79.3 us -> 75.4 us (0.951)
  Pallas kernels: 71.8 us -> 67.9 us
    pallas_call x1, Pallas kernels: 71.8 us -> 67.9 us  [body(): pl.pallas_call(functools.partial(kernel, n_row, n_col, per, block, width,...]
where the time goes in v4:
time: 75.4 us; the launch traced here: 75.1 us
  Pallas kernels  67.9 us (90%)
  local copies, waits for them, and re-layouts  4.7 us (6%)
  between operations  2.58 us (3%)
    pallas_call x1, Pallas kernels, body(): pl.pallas_call(functools.partial(kernel, n_row, n_col, per, block, width,...  67.9 us
    unnamed x3, local copies, waits for them, and re-layouts  4.7 us

profile of v4, /device:TPU:0, one launch (start us, length us, event | category | flops | bytes accessed | tf_op | source)
XLA Modules:
  0.0 75.1 jit_solution(4659989037919385602)
XLA Ops:
  2.6 1.4 %copy.8.pairs = s32[1,24,2]{2,1,0:T(8,128)} copy(s32[1,24,2]{1,2,0:T(2,128)} %param.8) | data formatting | bytes 384 | tf_op args[2]
  3.9 67.9 %shard_map.77 = (bf16[1024,128]{1,0:T(8,128)(2,1)}, bf16[1024,128]{1,0:T(8,128)(2,1)}) custom-call(s32[1,24,2]{2,1,0:T(8,128)} %copy.8.pairs, s32[1]{0:T(128)S(6)} %copy.11.count, f32[1]{0:T(128)S(6)} %copy.12.cut, f32[1]{0:T(128)S(6)} %copy.13.top, bf16[1024,128]{1,0:T(8,128)(2,1)} %v_ref.1, bf16[24,512,512]{2,1,0:T(8,128)(2,1)} %t_hbm.1), custom_call_target="tpu_custom_call" | custom-call | tf_op jit(solution)/shard_map/pallas_call | solution.py:440
  71.8 1.7 %copy.14 = bf16[1024,128]{1,0:T(8,128)(2,1)} copy(bf16[1024,128]{1,0:T(8,128)(2,1)} %get-tuple-element.4) | data formatting | bytes 524288
  73.5 1.7 %copy.15 = bf16[1024,128]{1,0:T(8,128)(2,1)} copy(bf16[1024,128]{1,0:T(8,128)(2,1)} %get-tuple-element.5) | data formatting | bytes 524288
